TPU v7x, 32 devices: a whole 2x2x4 slice. The times are simulated.
32 devices in a mesh: tp: 8 (over y, x, core), sp: 4 (over z).
Axes of the slice: x: 2, y: 2, z: 4, core: 2. Of those that a mesh axis runs over, the one named last changes fastest.
Arguments:
- inputs: bfloat16 [256, 8192], P('tp', 'sp'), may hold values from -6 to 6
- out_grad: bfloat16 [256, 8192], P('sp', 'tp'), may hold values from -6 to 6
- gate_pre: bfloat16 [256, 28672], P(None, 'tp'), may hold values from -6 to 6
- up_pre: bfloat16 [256, 28672], P(None, 'tp'), may hold values from -6 to 6
- w_gate: bfloat16 [8192, 28672], P('sp', 'tp'), may hold values from -0.0625 to 0.0625
- w_up: bfloat16 [8192, 28672], P('sp', 'tp'), may hold values from -0.0625 to 0.0625
- w_down: bfloat16 [28672, 8192], P('tp', 'sp'), may hold values from -0.03125 to 0.03125
Outputs:
- grad_input: bfloat16 [256, 8192], P('tp', 'sp')
- grad_gate: bfloat16 [8192, 28672], P('sp', 'tp')
- grad_up: bfloat16 [8192, 28672], P('sp', 'tp')
- grad_down: bfloat16 [28672, 8192], P('tp', 'sp')
All inputs are finite; a program needn't handle non-finite values.
Results may differ from a plain program's by a relative error of at most 0.0049.
Values may be sent and summed in bfloat16 or wider, within the bound.
A program may use at most 192 MiB of HBM per device.

v0:
```python
import jax
import jax.numpy as jnp
from jax import lax
from jax.sharding import PartitionSpec as P


def swiglu_back(hidden_grad, gate_pre, up_pre):
    gate = gate_pre.astype(jnp.float32)
    upward = up_pre.astype(jnp.float32)
    sigmoid = jax.nn.sigmoid(gate)
    up_grad = (hidden_grad * gate * sigmoid).astype(jnp.bfloat16)
    gate_grad = (hidden_grad * upward * sigmoid * (1.0 + gate * (1.0 - sigmoid))).astype(
        jnp.bfloat16
    )
    return (gate_grad, up_grad)


def rows_times(grads, weight):
    return lax.dot_general(
        grads, weight, (((1,), (1,)), ((), ())), preferred_element_type=jnp.float32
    )


def per_device(inputs, out_grad, gate_pre, up_pre, w_gate, w_up, w_down):
    wide_rows = lax.all_gather(out_grad, "tp", axis=1, tiled=True)
    regrouped = lax.all_to_all(wide_rows, "sp", split_axis=1, concat_axis=0, tiled=True)
    gate = gate_pre.astype(jnp.float32)
    hidden = (gate * jax.nn.sigmoid(gate) * up_pre.astype(jnp.float32)).astype(jnp.bfloat16)
    grad_down = lax.dot_general(
        hidden, regrouped, (((0,), (0,)), ((), ())), preferred_element_type=jnp.float32
    ).astype(jnp.bfloat16)
    partial_grad = lax.dot_general(
        regrouped, w_down, (((1,), (1,)), ((), ())), preferred_element_type=jnp.float32
    )
    hidden_grad = lax.psum(partial_grad, "sp")
    gate_grad, up_grad = swiglu_back(hidden_grad, gate_pre, up_pre)
    dims = (((0,), (0,)), ((), ()))
    piece = lax.all_gather(inputs, "tp", axis=0, tiled=True)
    new_gate = lax.dot_general(piece, gate_grad, dims, preferred_element_type=jnp.float32)
    new_up = lax.dot_general(piece, up_grad, dims, preferred_element_type=jnp.float32)
    via_gate = lax.psum_scatter(
        rows_times(gate_grad, w_gate), "tp", scatter_dimension=0, tiled=True
    )
    via_up = lax.psum_scatter(rows_times(up_grad, w_up), "tp", scatter_dimension=0, tiled=True)
    total = via_gate + via_up
    return (
        total.astype(jnp.bfloat16),
        new_gate.astype(jnp.bfloat16),
        new_up.astype(jnp.bfloat16),
        grad_down,
    )


def solution(mesh):
    in_specs = (
        P("tp", "sp"),
        P("sp", "tp"),
        P(None, "tp"),
        P(None, "tp"),
        P("sp", "tp"),
        P("sp", "tp"),
        P("tp", "sp"),
    )
    out_specs = (P("tp", "sp"), P("sp", "tp"), P("sp", "tp"), P("tp", "sp"))
    return jax.shard_map(
        per_device, mesh=mesh, in_specs=in_specs, out_specs=out_specs, check_vma=False
    )
```

profile of v0, /device:TPU:0, one launch (start us, length us, event | category | flops | bytes accessed | tf_op | source)
XLA Modules:
  0.0 316.0 jit_solution(610266666883076665)
XLA Ops:
  7.2 0.0 all-gather.3.cloned.1.call-start
  7.2 0.7 all-gather.3.cloned.1.call-update
  7.9 0.0 all-reduce.2.cloned.1.call-start
  7.9 28.2 %all-gather.3.cloned.1.call-done = bf16[64,8192]{1,0:T(8,128)(2,1)} async-done(((bf16[64,1024]{1,0:T(8,128)(2,1)}), bf16[64,8192]{1,0:T(8,128)(2,1)}) %all-gather.3.cloned.1.call-update) | async-done | bytes 1048592 | tf_op jit(solution)/shard_map/all_gather | solution.py:25
  36.1 1.3 copy.23
  37.4 30.6 %all_to_all.19 = bf16[64,4,2048]{2,0,1:T(8,128)(2,1)S(1)} all-to-all(bf16[64,4,2048]{2,0,1:T(8,128)(2,1)S(1)} %bitcast.20), channel_id=1, replica_groups=mesh['tp'=8,'sp'=4] {'sp'}, dimensions={1} | all-to-all | bytes 2097152 | tf_op jit(solution)/shard_map/all_to_all | solution.py:26
  68.0 9.1 %fusion.17 = f32[256,3584]{1,0:T(8,128)} fusion(bf16[256,2048]{1,0:T(8,128)(2,1)S(1)} %bitcast.21, bf16[3584,2048]{1,0:T(8,128)(2,1)} %param.13), kind=kOutput, calls=%fused_computation.25 | convolution fusion | flops 3758096384 | bytes 19398656 | tf_op jit(solution)/shard_map/dot_general | solution.py:32
  77.1 0.0 all-reduce.2.cloned.1.call-update
  77.1 0.0 all-gather.5.cloned.1.call-start
  77.2 0.7 all-gather.5.cloned.1.call-update
  77.9 0.0 reduce-scatter.2.cloned.1.call-start
  77.9 135.5 %all-reduce.2.cloned.1.call-done = f32[256,3584]{1,0:T(8,128)} async-done(((f32[256,3584]{1,0:T(8,128)}), f32[256,3584]{1,0:T(8,128)}) %all-reduce.2.cloned.1.call-update) | async-done | bytes 3670032 | tf_op jit(solution)/shard_map/psum | solution.py:35
  213.5 4.6 %fusion.4 = bf16[256,3584]{1,0:T(8,128)(2,1)S(1)} fusion(f32[256,3584]{1,0:T(8,128)} %all-reduce.2.cloned.1.call-done, bf16[256,3584]{1,0:T(8,128)(2,1)} %param.10, bf16[256,3584]{1,0:T(8,128)(2,1)} %param.9), kind=kLoop, calls=%fused_computation.13 | loop fusion | flops 11010048 | bytes 9175040 | tf_op jit(solution)/shard_map/convert_element_type | solution.py:12
  218.1 8.9 %fusion.18 = f32[256,2048]{1,0:T(8,128)} fusion(bf16[256,3584]{1,0:T(8,128)(2,1)S(1)} %fusion.4, bf16[2048,3584]{1,0:T(8,128)(2,1)} %param.11), kind=kOutput, calls=%fused_computation.26 | convolution fusion | flops 3758096384 | bytes 18612224 | tf_op jit(solution)/shard_map/dot_general | solution.py:19
  227.1 12.9 %convolution_add_fusion = f32[256,2048]{1,0:T(8,128)} fusion(f32[256,2048]{1,0:T(8,128)} %fusion.18, bf16[2048,3584]{1,0:T(8,128)(2,1)} %param.12, f32[256,3584]{1,0:T(8,128)} %all-reduce.2.cloned.1.call-done, bf16[256,3584]{1,0:T(8,128)(2,1)} %param.9), kind=kOutput, calls=%fused_computation.21 | convolution fusion | flops 3765043200 | bytes 24379392 | tf_op jit(solution)/shard_map/dot_general | solution.py:19
  240.0 0.0 reduce-scatter.2.cloned.1.call-update
  240.0 10.3 %convolution_convert_fusion = bf16[3584,2048]{1,0:T(8,128)(2,1)} fusion(bf16[256,2048]{1,0:T(8,128)(2,1)S(1)} %bitcast.22, bf16[256,3584]{1,0:T(8,128)(2,1)} %param.10, bf16[256,3584]{1,0:T(8,128)(2,1)} %param.9), kind=kOutput, calls=%fused_computation | convolution fusion | flops 3772776448 | bytes 19398656 | tf_op jit(solution)/shard_map/dot_general | solution.py:29
  250.3 0.0 all-gather.5.cloned.1.call-done
  250.3 12.9 %fusion.1 = bf16[2048,3584]{0,1:T(8,128)(2,1)} fusion(bf16[256,2048]{1,0:T(8,128)(2,1)} %all-gather.5.cloned.1.call-done, f32[256,3584]{1,0:T(8,128)} %all-reduce.2.cloned.1.call-done, bf16[256,3584]{1,0:T(8,128)(2,1)} %param.9), kind=kOutput, calls=%fused_computation.4 | convolution fusion | flops 3771858944 | bytes 21233664 | tf_op jit(solution)/shard_map/dot_general | solution.py:40
  263.2 0.0 copy-start
  263.2 18.8 %copy.20 = bf16[2048,3584]{1,0:T(8,128)(2,1)} copy(bf16[2048,3584]{0,1:T(8,128)(2,1)} %fusion.1) | data formatting | bytes 29360128
  281.9 0.0 copy-done
  281.9 7.3 %fusion = bf16[2048,3584]{0,1:T(8,128)(2,1)} fusion(bf16[256,3584]{1,0:T(8,128)(2,1)S(1)} %fusion.4, bf16[256,2048]{1,0:T(8,128)(2,1)S(1)} %copy-done), kind=kOutput, calls=%fused_computation.3 | convolution fusion | flops 3765436416 | bytes 17563648 | tf_op jit(solution)/shard_map/dot_general | solution.py:39
  289.2 18.6 %copy.19 = bf16[2048,3584]{1,0:T(8,128)(2,1)} copy(bf16[2048,3584]{0,1:T(8,128)(2,1)} %fusion) | data formatting | bytes 29360128
  307.9 0.0 reduce-scatter.2.cloned.1.call-done
  307.9 1.6 convert_element_type.39
Async XLA Ops:
  7.2 29.0 %all-gather.3.cloned.1.call-start = ((), (), s32[]{:S(2)}) async-start(), calls=%async_computation.2 | async-start | bytes 1179648 | tf_op jit(solution)/shard_map/all_gather | solution.py:25
  7.9 205.6 %all-reduce.2.cloned.1.call-start = ((), (), s32[]{:S(2)}) async-start(), calls=%async_computation.3 | async-start | bytes 7340032 | tf_op jit(solution)/shard_map/psum | solution.py:35
  77.1 173.1 %all-gather.5.cloned.1.call-start = ((), (), s32[]{:S(2)}) async-start(), calls=%async_computation.4 | async-start | bytes 1179648 | tf_op jit(solution)/shard_map/all_gather | solution.py:38
  77.9 230.0 %reduce-scatter.2.cloned.1.call-start = ((), (), s32[]{:S(2)}) async-start(), calls=%async_computation.5 | async-start | bytes 2359296 | tf_op jit(solution)/shard_map/reduce_scatter | solution.py:41
  263.2 18.8 %copy-start = (bf16[256,2048]{1,0:T(8,128)(2,1)S(1)}, bf16[256,2048]{1,0:T(8,128)(2,1)}, u32[]{:S(2)}) copy-start(bf16[256,2048]{1,0:T(8,128)(2,1)} %all-gather.5.cloned.1.call-done) | copy-start | bytes 3145732
Sparse Core Ops, SparseCore 0:
  9.9 26.1 all-gather.2
  77.3 136.1 all-reduce.1
  215.4 22.4 all-gather.4
  241.0 41.1 reduce-scatter.1
where the time goes:
time: 317 us; the launch traced here: 316 us
  waiting for transfers between devices  165 us (52%)
  matrix products  61.5 us (19%)
  local copies, waits for them, and re-layouts  38.7 us (12%)
  blocking collectives  30.6 us (10%)
  between operations  13.8 us (4%)
  other arithmetic  6.26 us (2%)
    psum x1, waiting for transfers between devices, per_device(): hidden_grad = lax.psum(partial_grad, 'sp')  136 us
    unnamed x4, local copies, waits for them, and re-layouts  37.4 us
    all_to_all x1, blocking collectives, per_device(): lax.all_to_all(wide_rows, 'sp', split_axis=1, concat_axis=0, tiled=True)  30.6 us
    all_gather x1, waiting for transfers between devices, per_device(): wide_rows = lax.all_gather(out_grad, 'tp', axis=1, tiled=True)  28.2 us
    dot_general x2, matrix products, rows_times(): lax.dot_general(grads, weight, (((1,), (1,)), ((), ())), preferred_elemen...  21.9 us
    dot_general x1, matrix products, per_device(): lax.dot_general(piece, up_grad, dims, preferred_element_type=jnp.float32)  12.9 us
    dot_general x1, matrix products, per_device(): lax.dot_general(hidden, regrouped, (((0,), (0,)), ((), ())), preferred_el...  10.3 us
    dot_general x1, matrix products, per_device(): lax.dot_general(regrouped, w_down, (((1,), (1,)), ((), ())), preferred_el...  9.13 us
  transfers between devices with their start and end apart: 4, of which 2 were waited for; matrix products, arithmetic and copies ran while one was open for 30% of the time, Pallas kernels for 0%

commit v1 on v0

--- a/solution.py
+++ b/solution.py
@@ -1,7 +1,20 @@
+import functools
 import jax
 import jax.numpy as jnp
 from jax import lax
 from jax.sharding import PartitionSpec as P
+
+
+def _treat_region(message, across):
+    dev_n = jax.lax.axis_size(across)
+    tmp = lambda m_next: [(dev, dev ^ m_next) for dev in range(dev_n)]
+    w1 = message
+    for dd in range(dev_n.bit_length() - 1):
+        w1 = w1 + jax.lax.ppermute(w1, across, tmp(1 << dd))
+    return w1
+
+
+types_wait = functools.partial(_treat_region, across="sp")
 
 
 def swiglu_back(hidden_grad, gate_pre, up_pre):
@@ -32,7 +45,7 @@
     partial_grad = lax.dot_general(
         regrouped, w_down, (((1,), (1,)), ((), ())), preferred_element_type=jnp.float32
     )
-    hidden_grad = lax.psum(partial_grad, "sp")
+    hidden_grad = types_wait(partial_grad)
     gate_grad, up_grad = swiglu_back(hidden_grad, gate_pre, up_pre)
     dims = (((0,), (0,)), ((), ()))
     piece = lax.all_gather(inputs, "tp", axis=0, tiled=True)

time: 317 us -> 417 us (1.32)
  waiting for transfers between devices: 165 us -> 267 us
  matrix products: 61.5 us -> 55 us
    ppermute x0 -> x2, waiting for transfers between devices: none -> 238 us  [_treat_region(): w1 = w1 + jax.lax.ppermute(w1, across, tmp(1 << dd))]
    psum x1 -> x0, waiting for transfers between devices: 136 us -> none  [per_device(): hidden_grad = lax.psum(partial_grad, 'sp')]
    dot_general x1, matrix products: 12.9 us -> 7.3 us  [per_device(): lax.dot_general(piece, up_grad, dims, preferred_element_type=jnp.float32)]
    unnamed x4 -> x6, local copies, waits for them, and re-layouts: 37.4 us -> 37.4 us
  transfers between devices with their start and end apart: 4 -> 5, of which waited for: 2 -> 3; matrix products, arithmetic and copies ran while one was open for 30% -> 22% of each run, Pallas kernels for 0% -> 0%
where the time goes in v1:
time: 417 us; the launch traced here: 416 us
  waiting for transfers between devices  267 us (64%)
  matrix products  55 us (13%)
  local copies, waits for them, and re-layouts  38.7 us (9%)
  blocking collectives  30.6 us (7%)
  between operations  13.8 us (3%)
  other arithmetic  9.24 us (2%)
    ppermute x2, waiting for transfers between devices, _treat_region(): w1 = w1 + jax.lax.ppermute(w1, across, tmp(1 << dd))  238 us
    unnamed x6, local copies, waits for them, and re-layouts  37.4 us
    all_to_all x1, blocking collectives, per_device(): lax.all_to_all(wide_rows, 'sp', split_axis=1, concat_axis=0, tiled=True)  30.6 us
    all_gather x1, waiting for transfers between devices, per_device(): wide_rows = lax.all_gather(out_grad, 'tp', axis=1, tiled=True)  28.2 us
    dot_general x2, matrix products, rows_times(): lax.dot_general(grads, weight, (((1,), (1,)), ((), ())), preferred_elemen...  18.8 us
    dot_general x1, matrix products, per_device(): lax.dot_general(piece, gate_grad, dims, preferred_element_type=jnp.float32)  11.4 us
    dot_general x1, matrix products, per_device(): lax.dot_general(hidden, regrouped, (((0,), (0,)), ((), ())), preferred_el...  10.2 us
  transfers between devices with their start and end apart: 5, of which 3 were waited for; matrix products, arithmetic and copies ran while one was open for 22% of the time, Pallas kernels for 0%

profile of v1, /device:TPU:0, one launch (start us, length us, event | category | flops | bytes accessed | tf_op | source)
XLA Modules:
  0.0 415.8 jit_solution(1893886229625268471)
XLA Ops:
  7.2 0.0 all-gather.3.cloned.1.call-start
  7.2 0.7 all-gather.3.cloned.1.call-update
  7.9 0.0 all-gather.5.cloned.1.call-start
  7.9 28.2 %all-gather.3.cloned.1.call-done = bf16[64,8192]{1,0:T(8,128)(2,1)} async-done(((bf16[64,1024]{1,0:T(8,128)(2,1)}), bf16[64,8192]{1,0:T(8,128)(2,1)}) %all-gather.3.cloned.1.call-update) | async-done | bytes 1048592 | tf_op jit(solution)/shard_map/all_gather | solution.py:38
  36.1 1.3 copy.23
  37.4 30.6 %all_to_all.19 = bf16[64,4,2048]{2,0,1:T(8,128)(2,1)S(1)} all-to-all(bf16[64,4,2048]{2,0,1:T(8,128)(2,1)S(1)} %bitcast.22), channel_id=1, replica_groups=mesh['tp'=8,'sp'=4] {'sp'}, dimensions={1} | all-to-all | bytes 2097152 | tf_op jit(solution)/shard_map/all_to_all | solution.py:39
  68.0 7.3 %fusion.16 = f32[256,3584]{1,0:T(8,128)S(1)} fusion(bf16[256,2048]{1,0:T(8,128)(2,1)S(1)} %bitcast.23, bf16[3584,2048]{1,0:T(8,128)(2,1)} %param.13), kind=kOutput, calls=%fused_computation.25 | convolution fusion | flops 3758096384 | bytes 19398656 | tf_op jit(solution)/shard_map/dot_general | solution.py:45
  75.3 0.3 collective-permute-start
  75.6 80.2 %collective-permute-done = f32[256,3584]{1,0:T(8,128)S(1)} collective-permute-done((f32[256,3584]{1,0:T(8,128)S(1)}, f32[256,3584]{1,0:T(8,128)S(1)}, u32[]{:S(2)}, u32[]{:S(2)}) %collective-permute-start) | collective-permute-done | bytes 3670048 | tf_op jit(solution)/shard_map/ppermute | solution.py:13
  155.8 2.4 add.20
  158.2 0.6 collective-permute-start.1
  158.8 0.0 all-gather.5.cloned.1.call-update
  158.8 0.2 reduce-scatter.2.cloned.1.call-start
  159.0 158.3 %collective-permute-done.1 = f32[256,3584]{1,0:T(8,128)} collective-permute-done((f32[256,3584]{1,0:T(8,128)}, f32[256,3584]{1,0:T(8,128)}, u32[]{:S(2)}, u32[]{:S(2)}) %collective-permute-start.1) | collective-permute-done | bytes 3670048 | tf_op jit(solution)/shard_map/ppermute | solution.py:13
  317.3 5.2 %fusion.11 = (bf16[256,3584]{1,0:T(8,128)(2,1)S(1)}, bf16[256,3584]{1,0:T(8,128)(2,1)S(1)}) fusion(bf16[256,3584]{1,0:T(8,128)(2,1)} %param.9, f32[256,3584]{1,0:T(8,128)} %add.20, f32[256,3584]{1,0:T(8,128)} %collective-permute-done.1, bf16[256,3584]{1,0:T(8,128)(2,1)} %param.10), kind=kLoop, calls=%fused_computation.20 | loop fusion | flops 14680064 | bytes 14680064 | tf_op jit(solution)/shard_map/convert_element_type | solution.py:24
  322.5 0.0 copy-start
  322.5 9.3 %fusion.17 = f32[256,2048]{1,0:T(8,128)} fusion(bf16[256,3584]{1,0:T(8,128)(2,1)S(1)} %get-tuple-element.20, bf16[2048,3584]{1,0:T(8,128)(2,1)} %param.12), kind=kOutput, calls=%fused_computation.26 | convolution fusion | flops 3758096384 | bytes 18612224 | tf_op jit(solution)/shard_map/dot_general | solution.py:32
  331.8 0.0 copy-done
  331.8 9.5 %fusion.15 = f32[256,2048]{1,0:T(8,128)} fusion(f32[256,2048]{1,0:T(8,128)} %fusion.17, bf16[256,3584]{1,0:T(8,128)(2,1)S(1)} %get-tuple-element.21, bf16[2048,3584]{1,0:T(8,128)(2,1)} %param.11), kind=kOutput, calls=%fused_computation.24 | convolution fusion | flops 3758620672 | bytes 20709376 | tf_op jit(solution)/shard_map/dot_general | solution.py:32
  341.3 0.0 reduce-scatter.2.cloned.1.call-update
  341.4 10.2 %convolution_convert_fusion = bf16[3584,2048]{1,0:T(8,128)(2,1)} fusion(bf16[256,2048]{1,0:T(8,128)(2,1)S(1)} %bitcast.24, bf16[256,3584]{1,0:T(8,128)(2,1)} %param.10, bf16[256,3584]{1,0:T(8,128)(2,1)} %param.9), kind=kOutput, calls=%fused_computation | convolution fusion | flops 3772776448 | bytes 19398656 | tf_op jit(solution)/shard_map/dot_general | solution.py:42
  351.6 0.0 all-gather.5.cloned.1.call-done
  351.6 11.4 %fusion = bf16[2048,3584]{0,1:T(8,128)(2,1)} fusion(bf16[256,3584]{1,0:T(8,128)(2,1)} %copy-done, bf16[256,2048]{1,0:T(8,128)(2,1)} %all-gather.5.cloned.1.call-done), kind=kOutput, calls=%fused_computation.3 | convolution fusion | flops 3765436416 | bytes 17563648 | tf_op jit(solution)/shard_map/dot_general | solution.py:52
  362.9 0.0 copy-start.1
  362.9 18.8 %copy.19 = bf16[2048,3584]{1,0:T(8,128)(2,1)} copy(bf16[2048,3584]{0,1:T(8,128)(2,1)} %fusion) | data formatting | bytes 29360128
  381.7 0.0 copy-done.1
  381.7 7.3 %fusion.1 = bf16[2048,3584]{0,1:T(8,128)(2,1)} fusion(bf16[256,3584]{1,0:T(8,128)(2,1)S(1)} %get-tuple-element.20, bf16[256,2048]{1,0:T(8,128)(2,1)S(1)} %copy-done.1), kind=kOutput, calls=%fused_computation.4 | convolution fusion | flops 3765436416 | bytes 17563648 | tf_op jit(solution)/shard_map/dot_general | solution.py:53
  389.0 18.6 %copy.20 = bf16[2048,3584]{1,0:T(8,128)(2,1)} copy(bf16[2048,3584]{0,1:T(8,128)(2,1)} %fusion.1) | data formatting | bytes 29360128
  407.6 0.0 reduce-scatter.2.cloned.1.call-done
  407.6 1.6 convert_element_type.39
Async XLA Ops:
  7.2 29.0 %all-gather.3.cloned.1.call-start = ((), (), s32[]{:S(2)}) async-start(), calls=%async_computation.2 | async-start | bytes 1179648 | tf_op jit(solution)/shard_map/all_gather | solution.py:38
  7.9 343.7 %all-gather.5.cloned.1.call-start = ((), (), s32[]{:S(2)}) async-start(), calls=%async_computation.3 | async-start | bytes 1179648 | tf_op jit(solution)/shard_map/all_gather | solution.py:51
  75.3 80.4 %collective-permute-start = (f32[256,3584]{1,0:T(8,128)S(1)}, f32[256,3584]{1,0:T(8,128)S(1)}, u32[]{:S(2)}, u32[]{:S(2)}) collective-permute-start(f32[256,3584]{1,0:T(8,128)S(1)} %fusion.16), channel_id=1, source_target_pairs={{0,1},{1,0},{2,3},{3,2},{4,5},{5,4},{6,7},{7,6},{8,9},{9,8},{10,11... | collective-permute-start | bytes 11010056 | tf_op jit(solution)/shard_map/ppermute | solution.py:13
  158.2 159.1 %collective-permute-start.1 = (f32[256,3584]{1,0:T(8,128)}, f32[256,3584]{1,0:T(8,128)}, u32[]{:S(2)}, u32[]{:S(2)}) collective-permute-start(f32[256,3584]{1,0:T(8,128)} %add.20), channel_id=1, source_target_pairs={{0,2},{1,3},{2,0},{3,1},{4,6},{5,7},{6,4},{7,5},{8,10},{9,11},{10,... | collective-permute-start | bytes 11010056 | tf_op jit(solution)/shard_map/ppermute | solution.py:13
  158.8 248.8 %reduce-scatter.2.cloned.1.call-start = ((), (), s32[]{:S(2)}) async-start(), calls=%async_computation.4 | async-start | bytes 2359296 | tf_op jit(solution)/shard_map/reduce_scatter | solution.py:54
  322.5 9.3 %copy-start = (bf16[256,3584]{1,0:T(8,128)(2,1)}, bf16[256,3584]{1,0:T(8,128)(2,1)S(1)}, u32[]{:S(2)}) copy-start(bf16[256,3584]{1,0:T(8,128)(2,1)S(1)} %get-tuple-element.21) | copy-start | bytes 5505028
  362.9 18.8 %copy-start.1 = (bf16[256,2048]{1,0:T(8,128)(2,1)S(1)}, bf16[256,2048]{1,0:T(8,128)(2,1)}, u32[]{:S(2)}) copy-start(bf16[256,2048]{1,0:T(8,128)(2,1)} %all-gather.5.cloned.1.call-done) | copy-start | bytes 3145732
Sparse Core Ops, SparseCore 0:
  9.9 26.1 all-gather.2
  158.9 22.4 all-gather.4
  341.5 39.9 reduce-scatter.1
